TPU v7x, 512 devices: a whole 4x4x16 slice. The times are simulated.
512 devices in a mesh: dx: 16 (over y, x), dy: 32 (over z, core).
Axes of the slice: x: 4, y: 4, z: 16, core: 2. Of those that a mesh axis runs over, the one named last changes fastest.
Arguments:
- audio: bfloat16 [32, 128, 2570], P('dy', 'dx'), may hold values from -6 to 6
- counts: int32 [32, 16], P('dy', 'dx'), may hold values from 1 to 8, 64 in all within a row
- cotangent: bfloat16 [32, 64, 256, 512], P('dy', 'dx'), may hold values from -6 to 6
- conv_first: bfloat16 [10, 512], replicated, may hold values from -2 to 2
- norm_gain: float32 [512], replicated, may hold values from 0.1 to 1.9
- norm_bias: float32 [512], replicated, may hold values from -3 to 3
- conv_second: bfloat16 [1536, 512], replicated, may hold values from -0.15625 to 0.15625
Outputs:
- grad_conv_first: float32 [10, 512], replicated
- grad_norm: float32 [2, 512], replicated
- grad_conv_second: float32 [1536, 512], P('dy')
Inputs may be any that keep to these rules, and one draw needn't show every extreme that they name: In each group along dy the counts sum to 64, and some device of each group holds exactly 8 live crops.
All inputs are finite; a program needn't handle non-finite values.
Results may differ from a plain program's by a relative error of at most 0.0051.
Values may be sent and summed in bfloat16 or wider, within the bound.
A program may use at most 128 MiB of HBM per device.

v0:
```python
import math
import jax
import jax.numpy as jnp
from jax import lax
from jax.sharding import PartitionSpec as P


def gelu_cdf(value):
    return 0.5 * (1.0 + lax.erf(value * 0.7071067811865476))


def gelu_slope(value):
    return gelu_cdf(value) + value * jnp.exp(-0.5 * value * value) * 0.3989422804014327


def forward_backward(
    crop_waves, cot_rows, conv_first, norm_gain, norm_bias, conv_second, loss_scale
):
    batch_size = crop_waves.shape[0]
    frames = cot_rows.shape[1]
    first_len = 2 * frames + 1
    channels = conv_second.shape[1]
    early_taps = crop_waves[:, : 5 * first_len].reshape(batch_size, first_len, 5)
    late_taps = crop_waves[:, 5 : 5 * first_len + 5].reshape(batch_size, first_len, 5)
    patches = jnp.concatenate([early_taps, late_taps], axis=2).reshape(batch_size * first_len, 10)
    pre_norm = jnp.dot(patches, conv_first, preferred_element_type=jnp.float32).reshape(
        batch_size, first_len, channels
    )
    centre = pre_norm - jnp.mean(pre_norm, axis=1, keepdims=True)
    inv_std = lax.rsqrt(jnp.mean(centre * centre, axis=1, keepdims=True) + 1e-05)
    normed = centre * inv_std
    shifted = normed * norm_gain + norm_bias
    hidden = (shifted * gelu_cdf(shifted)).astype(jnp.bfloat16)
    two_taps = hidden[:, : 2 * frames].reshape(batch_size, frames, 2 * channels)
    third_tap = hidden[:, 2::2]
    second_rows = jnp.concatenate([two_taps, third_tap], axis=2).reshape(
        batch_size * frames, 3 * channels
    )
    pre_act = jnp.dot(second_rows, conv_second, preferred_element_type=jnp.float32)
    grad_rows = (
        loss_scale
        * cot_rows.reshape(batch_size * frames, channels).astype(jnp.float32)
        * gelu_slope(pre_act)
    ).astype(jnp.bfloat16)
    grad_cols = jnp.dot(grad_rows, conv_second.T, preferred_element_type=jnp.float32).reshape(
        batch_size, frames, 3 * channels
    )
    first_taps = grad_cols[:, :, : 2 * channels].reshape(batch_size, 2 * frames, channels)
    late_tap = jnp.stack(
        [grad_cols[:, :, 2 * channels :], jnp.zeros((batch_size, frames, channels), jnp.float32)],
        axis=2,
    ).reshape(batch_size, 2 * frames, channels)
    grad_hidden = jnp.concatenate(
        [first_taps, jnp.zeros((batch_size, 1, channels), jnp.float32)], axis=1
    )
    grad_hidden = grad_hidden + jnp.concatenate(
        [jnp.zeros((batch_size, 2, channels), jnp.float32), late_tap[:, : 2 * frames - 1]], axis=1
    )
    grad_shift = grad_hidden * gelu_slope(shifted)
    gain_grad = jnp.sum(grad_shift * normed, axis=(0, 1))
    shift_grad = jnp.sum(grad_shift, axis=(0, 1))
    grad_scaled = grad_shift * norm_gain
    grad_pre = inv_std * (
        grad_scaled
        - jnp.mean(grad_scaled, axis=1, keepdims=True)
        - normed * jnp.mean(grad_scaled * normed, axis=1, keepdims=True)
    )
    grad_pre = grad_pre.astype(jnp.bfloat16).reshape(batch_size * first_len, channels)
    grad_first = jnp.dot(patches.T, grad_pre, preferred_element_type=jnp.float32)
    return (second_rows, grad_rows, grad_first, jnp.stack([gain_grad, shift_grad]))


def on_device(audio, counts, cotangent, conv_first, norm_gain, norm_bias, conv_second):
    groups = lax.axis_size("dx")
    position = lax.axis_index("dx")
    slot_count = audio.shape[1]
    receive = cotangent.shape[1]
    frames = cotangent.shape[2]
    all_counts = lax.all_gather(counts, "dx", axis=1, tiled=True)[0]
    starts = jnp.cumsum(all_counts, dtype=jnp.int32) - all_counts
    everything = lax.all_gather(audio, "dx", axis=1, tiled=True)[0]
    wanted = jnp.arange(receive, dtype=jnp.int32) * groups + position
    holder = (
        jnp.sum((starts[None, :] <= wanted[:, None]).astype(jnp.int32), axis=1, dtype=jnp.int32) - 1
    )
    offset = wanted - starts[holder]
    crop_waves = jnp.take(everything, holder * slot_count + offset, axis=0)
    loss_scale = 1.0 / math.sqrt(groups * lax.axis_size("dy") * receive * frames)
    second_rows, grad_rows, grad_first, grad_gains = forward_backward(
        crop_waves, cotangent[0], conv_first, norm_gain, norm_bias, conv_second, loss_scale
    )
    row_share = conv_second.shape[0] // lax.axis_size("dy")
    grad_second = jnp.dot(second_rows.T, grad_rows, preferred_element_type=jnp.float32)
    summed_first, summed_gains, whole_second = lax.psum(
        (grad_first, grad_gains, grad_second), ("dx", "dy")
    )
    summed_second = lax.dynamic_slice_in_dim(
        whole_second, lax.axis_index("dy") * row_share, row_share, 0
    )
    return (summed_first, summed_gains, summed_second)


def solution(mesh):
    in_specs = (P("dy", "dx", None), P("dy", "dx"), P("dy", "dx", None, None), P(), P(), P(), P())
    out_specs = (P(), P(), P("dy", None))
    return jax.shard_map(
        on_device, mesh=mesh, in_specs=in_specs, out_specs=out_specs, check_vma=False
    )
```

profile of v0, /device:TPU:2, one launch (start us, length us, event | category | flops | bytes accessed | tf_op | source)
XLA Modules:
  0.0 583.2 jit_solution(14442549444901075429)
XLA Ops:
  7.2 0.0 copy-start
  7.2 0.0 all-reduce.7.cloned.1.call-start
  8.0 1.3 dynamic-slice
  9.3 0.7 bitcast_dynamic-update-slice_fusion
  9.9 15.7 %all-reduce.3 = s32[16]{0:T(128)S(1)} all-reduce(s32[16]{0:T(128)S(1)} %bitcast_dynamic-update-slice_fusion), channel_id=1, replica_groups=mesh['dx'=16,'dy'=32] {'dx'}, use_global_device_ids=true, to_apply=%add.3 | all-reduce | flops 16 | bytes 128 | tf_op jit(solution)/shard_map/squeeze | solution.py:79
  25.6 0.1 copy.14
  25.7 0.1 reduce
  25.9 0.2 convert_reduce_fusion
  26.1 0.6 gather_fusion
  26.8 24.8 %all_gather.7 = bf16[1,128,2570]{2,1,0:T(8,128)(2,1)S(1)} all-gather(bf16[1,8,2570]{2,1,0:T(8,128)(2,1)} %param.7), channel_id=1, replica_groups=mesh['dx'=16,'dy'=32] {'dx'}, dimensions={1}, use_global_device_ids=true | all-gather | bytes 699040 | tf_op jit(solution)/shard_map/all_gather | solution.py:81
  51.5 0.6 gather_fusion.1
  52.1 0.1 broadcast_select_fusion
  52.2 0.1 fusion.26
  52.3 0.4 reshape.141
  52.7 0.3 copy.15
  53.0 0.4 reshape.142
  53.4 0.3 copy.16
  53.7 0.0 copy-start.5
  53.7 0.0 copy-start.6
  53.7 1.5 fusion.27
  55.2 0.0 copy-start.1
  55.2 0.6 multiply_reduce_fusion.2
  55.8 1.3 copy-done.1
  57.1 0.0 copy-done.5
  57.2 0.0 copy-done.6
  57.2 2.4 multiply_convert_fusion.1
  59.6 0.0 copy-start.3
  59.6 11.7 %slice.24 = bf16[4,256,512]{2,1,0:T(8,128)(2,1)} slice(bf16[4,513,512]{2,1,0:T(8,128)(2,1)} %multiply_convert_fusion.1), slice={[0:4:1], [2:513:2], [0:512:1]} | slice | bytes 2097152 | tf_op jit(solution)/shard_map/slice | solution.py:35
  71.2 3.1 slice.34
  74.3 0.0 copy-done.3
  74.3 1.6 convert_multiply_fusion
  75.9 4.1 concatenate.20
  80.0 0.0 copy-done
  80.0 0.0 copy-start.2
  80.0 0.0 copy-start.4
  80.0 5.1 fusion.11
  85.1 0.0 copy-done.2
  85.1 0.0 copy-done.4
  85.1 3.6 fusion.12
  88.6 0.0 all-reduce.7.cloned.1.call-update
  88.7 1.8 fusion.28
  90.5 1.5 slice.36
  92.0 2.4 slice.35
  94.4 4.9 reshape.144
  99.3 3.0 stack.15
  102.4 3.4 stack.16
  105.7 0.0 slice-start
  105.7 6.1 %reshape.145 = f32[4,512,512]{2,1,0:T(8,128)} reshape(f32[4,256,2,512]{3,2,1,0:T(2,128)} %stack.16) | data formatting | bytes 8388608 | tf_op jit(solution)/shard_map/reshape | solution.py:52
  111.8 0.0 slice-start.1
  111.8 7.3 %multiply_reduce_fusion = (f32[512]{0:T(512)S(1)}, f32[4,512]{1,0:T(4,128)S(1)}, f32[4,512]{1,0:T(4,128)S(1)}, f32[512]{0:T(512)S(1)}, f32[4,513,512]{2,1,0:T(8,128)S(1)}) fusion(f32[4,512]{1,0:T(4,128)S(1)} %add_rsqrt_fusion, f32[4,513,512]{2,1,0:T(8,128)} %copy-done.1, f32[4,512]{1,0:T(4,128)S(1)} %broadcast_multiply_fusion.2, f32[512]{0:T(512)S(1)} %copy-done.5, ...), kind=kLoop, calls=%fused_computation.8 | loop fusion | flops 22057984 | bytes 16826368 | tf_op jit(solution)/shard_map/reduce_sum | solution.py:60
  119.2 0.0 slice-done
  119.2 0.0 slice-done.1
  119.2 1.4 fusion.14
  120.6 105.0 %all-reduce.4 = (f32[10,512]{1,0:T(8,128)}, f32[2,512]{1,0:T(2,128)}) all-reduce(f32[10,512]{1,0:T(8,128)S(1)} %fusion.14, f32[2,512]{1,0:T(2,128)S(1)} %pad_maximum_fusion.8), channel_id=1, replica_groups=mesh['dx'=16,'dy'=32] {'dx','dy'}, use_global_device_ids=true, to_apply=%region_6.7 | all-reduce | flops 6144 | bytes 49152 | tf_op jit(solution)/shard_map/psum | solution.py:94
  225.6 349.2 %all-reduce.7.cloned.1.call-done = f32[1536,512]{1,0:T(8,128)} async-done(((f32[1536,512]{1,0:T(8,128)}), f32[1536,512]{1,0:T(8,128)}) %all-reduce.7.cloned.1.call-update) | async-done | bytes 3145744 | tf_op jit(solution)/shard_map/psum | solution.py:94
  574.9 1.5 constant_dynamic-slice_fusion
  (15 shorter events, 0.1 us)
Async XLA Ops:
  7.2 72.8 %copy-start = (bf16[1536,512]{1,0:T(8,128)(2,1)S(1)}, bf16[1536,512]{1,0:T(8,128)(2,1)}, u32[]{:S(2)}) copy-start(bf16[1536,512]{1,0:T(8,128)(2,1)} %param.13) | copy-start | bytes 4718596
  7.2 567.7 %all-reduce.7.cloned.1.call-start = ((), (), s32[]{:S(2)}) async-start(), calls=%async_computation | async-start | bytes 6291456 | tf_op jit(solution)/shard_map/psum | solution.py:94
  53.7 3.5 copy-start.5
  53.7 3.5 copy-start.6
  55.2 2.0 copy-start.1
  59.6 14.7 %copy-start.3 = (bf16[1,4,256,512]{3,2,1,0:T(8,128)(2,1)S(1)}, bf16[1,4,256,512]{3,2,1,0:T(8,128)(2,1)}, u32[]{:S(2)}) copy-start(bf16[1,4,256,512]{3,2,1,0:T(8,128)(2,1)} %param.9) | copy-start | bytes 3145732
  80.0 5.1 copy-start.2
  80.0 5.1 copy-start.4
  105.7 13.5 %slice-start = ((s8[4259840]{0:T(1024)(128)(4,1)}), s8[65536]{0:T(1024)(128)(4,1)S(1)}, s32[]{:S(2)}) async-start(s8[4259840]{0:T(1024)(128)(4,1)} %bitcast.48), calls=%async_computation.1 | async-start | bytes 131072
  111.8 7.4 %slice-start.1 = ((s8[4259840]{0:T(1024)(128)(4,1)}), s8[4194304]{0:T(1024)(128)(4,1)S(1)}, s32[]{:S(2)}) async-start(s8[4259840]{0:T(1024)(128)(4,1)} %bitcast.48), calls=%async_computation.2 | async-start | bytes 8388608
Sparse Core Ops, SparseCore 0:
  88.8 486.0 all-reduce.6
where the time goes:
time: 584 us; the launch traced here: 583 us
  waiting for transfers between devices  349 us (60%)
  blocking collectives  145 us (25%)
  local copies, waits for them, and re-layouts  47.7 us (8%)
  between operations  15 us (3%)
  matrix products  13.3 us (2%)
  other arithmetic  12.4 us (2%)
    psum x1, waiting for transfers between devices, on_device(): lax.psum((grad_first, grad_gains, grad_second), ('dx', 'dy'))  349 us
    psum x1, blocking collectives, on_device(): lax.psum((grad_first, grad_gains, grad_second), ('dx', 'dy'))  105 us
    all_gather x1, blocking collectives, on_device(): everything = lax.all_gather(audio, 'dx', axis=1, tiled=True)[0]  24.8 us
    squeeze x1, blocking collectives, on_device(): all_counts = lax.all_gather(counts, 'dx', axis=1, tiled=True)[0]  15.7 us
  transfers between devices with their start and end apart: 1, of which 1 were waited for; matrix products, arithmetic and copies ran while one was open for 5% of the time, Pallas kernels for 0%

commit v1 on v0

--- a/solution.py
+++ b/solution.py
@@ -3,6 +3,27 @@
 import jax.numpy as jnp
 from jax import lax
 from jax.sharding import PartitionSpec as P
+
+
+def ring_gather(x, axis, dim):
+    peers, index, span = (lax.axis_size(axis), lax.axis_index(axis), x.shape[dim])
+    right = [(i, (i + 1) % peers) for i in range(peers)]
+    left = [(i, (i - 1) % peers) for i in range(peers)]
+    out = jnp.zeros((*x.shape[:dim], peers * span, *x.shape[dim + 1 :]), x.dtype)
+    out = lax.dynamic_update_slice_in_dim(out, x, index * span, axis=dim)
+    from_left = from_right = x
+    half = peers // 2
+    for step in range(1, half + 1):
+        from_left = lax.ppermute(from_left, axis, right)
+        out = lax.dynamic_update_slice_in_dim(
+            out, from_left, (index - step) % peers * span, axis=dim
+        )
+        if step < peers - half:
+            from_right = lax.ppermute(from_right, axis, left)
+            out = lax.dynamic_update_slice_in_dim(
+                out, from_right, (index + step) % peers * span, axis=dim
+            )
+    return out
 
 
 def gelu_cdf(value):
@@ -78,7 +99,7 @@
     frames = cotangent.shape[2]
     all_counts = lax.all_gather(counts, "dx", axis=1, tiled=True)[0]
     starts = jnp.cumsum(all_counts, dtype=jnp.int32) - all_counts
-    everything = lax.all_gather(audio, "dx", axis=1, tiled=True)[0]
+    everything = ring_gather(audio, "dx", 1)[0]
     wanted = jnp.arange(receive, dtype=jnp.int32) * groups + position
     holder = (
         jnp.sum((starts[None, :] <= wanted[:, None]).astype(jnp.int32), axis=1, dtype=jnp.int32) - 1

time: 584 us -> 642 us (1.099)
  starting transfers between devices: 0.04 us -> 58.8 us
  blocking collectives: 145 us -> 124 us
  waiting for transfers between devices: 349 us -> 368 us
    ppermute x0 -> x15, starting transfers between devices: none -> 58.7 us  [the longest x7 40.9 us: ring_gather(): from_right = lax.ppermute(from_right, axis, left)]
    all_gather x1 -> x0, blocking collectives: 24.8 us -> none  [on_device(): everything = lax.all_gather(audio, 'dx', axis=1, tiled=True)[0]]
    ppermute x0 -> x15, waiting for transfers between devices: none -> 15 us  [the longest x8 14.8 us: ring_gather(): from_left = lax.ppermute(from_left, axis, right)]
  transfers between devices with their start and end apart: 1 -> 16, of which waited for: 1 -> 5; matrix products, arithmetic and copies ran while one was open for 5% -> 5% of each run, Pallas kernels for 0% -> 0%
where the time goes in v1:
time: 642 us; the launch traced here: 641 us
  waiting for transfers between devices  368 us (57%)
  blocking collectives  124 us (19%)
  starting transfers between devices  58.8 us (9%)
  local copies, waits for them, and re-layouts  47.5 us (7%)
  between operations  15.4 us (2%)
  other arithmetic  13.7 us (2%)
  matrix products  13.4 us (2%)
    psum x1, waiting for transfers between devices, on_device(): lax.psum((grad_first, grad_gains, grad_second), ('dx', 'dy'))  353 us
    psum x1, blocking collectives, on_device(): lax.psum((grad_first, grad_gains, grad_second), ('dx', 'dy'))  109 us
    ppermute x7, starting transfers between devices, ring_gather(): from_right = lax.ppermute(from_right, axis, left)  40.9 us
    ppermute x8, starting transfers between devices, ring_gather(): from_left = lax.ppermute(from_left, axis, right)  17.9 us
    squeeze x1, blocking collectives, on_device(): all_counts = lax.all_gather(counts, 'dx', axis=1, tiled=True)[0]  15.3 us
    ppermute x8, waiting for transfers between devices, ring_gather(): from_left = lax.ppermute(from_left, axis, right)  14.8 us
  transfers between devices with their start and end apart: 16, of which 5 were waited for; matrix products, arithmetic and copies ran while one was open for 5% of the time, Pallas kernels for 0%

profile of v1, /device:TPU:2, one launch (start us, length us, event | category | flops | bytes accessed | tf_op | source)
XLA Modules:
  0.0 640.9 jit_solution(16892504022658934148)
XLA Ops:
  7.2 0.0 copy-start
  7.2 0.0 copy-start.3
  7.2 0.0 all-reduce.7.cloned.1.call-start
  7.2 8.0 %collective-permute-start.1 = (bf16[1,8,2570]{2,1,0:T(8,128)(2,1)}, bf16[1,8,2570]{2,1,0:T(8,128)(2,1)S(1)}, u32[]{:S(2)}, u32[]{:S(2)}) collective-permute-start(bf16[1,8,2570]{2,1,0:T(8,128)(2,1)} %param.7), channel_id=1, source_target_pairs={{0,480},{32,0},{64,32},{96,64},{128,96},{160,128},{192,160},{224,1... | collective-permute-start | bytes 123368 | tf_op jit(solution)/shard_map/ppermute | solution.py:22
  15.8 1.3 dynamic-slice
  17.1 0.7 bitcast_dynamic-update-slice_fusion.16
  17.8 1.9 collective-permute-start
  19.7 15.3 %all-reduce.3 = s32[16]{0:T(128)S(1)} all-reduce(s32[16]{0:T(128)S(1)} %bitcast_dynamic-update-slice_fusion.16), channel_id=1, replica_groups=mesh['dx'=16,'dy'=32] {'dx'}, use_global_device_ids=true, to_apply=%add.3 | all-reduce | flops 16 | bytes 128 | tf_op jit(solution)/shard_map/squeeze | solution.py:100
  35.0 0.1 copy.14
  35.1 0.1 reduce
  35.3 0.2 convert_reduce_fusion
  35.5 0.6 gather_fusion
  36.1 2.9 convert_multiply_fusion
  39.4 2.5 collective-permute-start.3
  42.0 3.3 collective-permute-start.2
  45.3 0.2 collective-permute-done.3
  45.5 2.8 collective-permute-start.5
  48.3 3.1 collective-permute-start.4
  51.4 0.0 collective-permute-done.5
  51.4 5.7 collective-permute-start.7
  57.1 0.0 collective-permute-done.4
  57.1 1.9 collective-permute-start.6
  59.1 7.2 %collective-permute-start.9 = (bf16[1,8,2570]{2,1,0:T(8,128)(2,1)S(1)}, bf16[1,8,2570]{2,1,0:T(8,128)(2,1)S(1)}, u32[]{:S(2)}, u32[]{:S(2)}) collective-permute-start(bf16[1,8,2570]{2,1,0:T(8,128)(2,1)S(1)} %collective-permute-done.7), channel_id=1, source_target_pairs={{0,480},{32,0},{64,32},{96,64},{128,96},{160,128},{192,160},{224,1... | collective-permute-start | bytes 123368 | tf_op jit(solution)/shard_map/ppermute | solution.py:22
  66.4 0.0 collective-permute-done.6
  66.4 1.9 collective-permute-start.8
  68.4 7.4 %collective-permute-start.11 = (bf16[1,8,2570]{2,1,0:T(8,128)(2,1)S(1)}, bf16[1,8,2570]{2,1,0:T(8,128)(2,1)S(1)}, u32[]{:S(2)}, u32[]{:S(2)}) collective-permute-start(bf16[1,8,2570]{2,1,0:T(8,128)(2,1)S(1)} %collective-permute-done.9), channel_id=1, source_target_pairs={{0,480},{32,0},{64,32},{96,64},{128,96},{160,128},{192,160},{224,1... | collective-permute-start | bytes 123368 | tf_op jit(solution)/shard_map/ppermute | solution.py:22
  75.8 0.2 collective-permute-done.8
  76.0 1.9 collective-permute-start.10
  78.0 7.2 %collective-permute-start.13 = (bf16[1,8,2570]{2,1,0:T(8,128)(2,1)S(1)}, bf16[1,8,2570]{2,1,0:T(8,128)(2,1)S(1)}, u32[]{:S(2)}, u32[]{:S(2)}) collective-permute-start(bf16[1,8,2570]{2,1,0:T(8,128)(2,1)S(1)} %collective-permute-done.11), channel_id=1, source_target_pairs={{0,480},{32,0},{64,32},{96,64},{128,96},{160,128},{192,160},{224,1... | collective-permute-start | bytes 123368 | tf_op jit(solution)/shard_map/ppermute | solution.py:22
  85.3 0.0 collective-permute-done.10
  85.3 1.9 collective-permute-start.12
  87.2 7.3 %collective-permute-done.12 = bf16[1,8,2570]{2,1,0:T(8,128)(2,1)S(1)} collective-permute-done((bf16[1,8,2570]{2,1,0:T(8,128)(2,1)S(1)}, bf16[1,8,2570]{2,1,0:T(8,128)(2,1)S(1)}, u32[]{:S(2)}, u32[]{:S(2)}) %collective-permute-start.12) | collective-permute-done | bytes 41152 | tf_op jit(solution)/shard_map/ppermute | solution.py:17
  94.5 1.9 collective-permute-start.14
  96.5 7.3 %collective-permute-done.14 = bf16[1,8,2570]{2,1,0:T(8,128)(2,1)S(1)} collective-permute-done((bf16[1,8,2570]{2,1,0:T(8,128)(2,1)S(1)}, bf16[1,8,2570]{2,1,0:T(8,128)(2,1)S(1)}, u32[]{:S(2)}, u32[]{:S(2)}) %collective-permute-start.14) | collective-permute-done | bytes 41152 | tf_op jit(solution)/shard_map/ppermute | solution.py:17
  103.7 0.6 gather_fusion.1
  104.3 0.1 broadcast_select_fusion
  104.4 0.1 fusion.26
  104.5 0.4 reshape.173
  104.9 0.3 copy.15
  105.2 0.4 reshape.174
  105.6 0.3 copy.16
  105.9 0.8 fusion.27
  106.7 0.6 multiply_reduce_fusion.2
  107.3 1.3 copy-done.1
  108.6 2.4 multiply_convert_fusion.1
  111.0 10.1 %slice.24 = bf16[4,256,512]{2,1,0:T(8,128)(2,1)S(1)} slice(bf16[4,513,512]{2,1,0:T(8,128)(2,1)} %multiply_convert_fusion.1), slice={[0:4:1], [2:513:2], [0:512:1]} | slice | bytes 2097152 | tf_op jit(solution)/shard_map/slice | solution.py:56
  121.2 3.1 slice.34
  124.3 4.1 concatenate.20
  128.3 4.7 fusion.11
  133.1 1.0 copy-done.7
  134.1 3.5 fusion.12
  137.6 3.0 fusion.28
  140.6 1.5 slice.36
  142.1 2.4 slice.35
  144.5 0.0 all-reduce.7.cloned.1.call-update
  144.5 5.0 reshape.176
  149.5 3.0 stack.15
  152.5 3.4 stack.16
  155.9 6.1 reshape.177
  162.0 7.3 %multiply_reduce_fusion = (f32[512]{0:T(512)S(1)}, f32[4,512]{1,0:T(4,128)S(1)}, f32[4,512]{1,0:T(4,128)S(1)}, f32[512]{0:T(512)S(1)}, f32[4,513,512]{2,1,0:T(8,128)S(1)}) fusion(f32[4,512]{1,0:T(4,128)S(1)} %add_rsqrt_fusion, f32[4,513,512]{2,1,0:T(8,128)} %copy-done.1, f32[4,512]{1,0:T(4,128)S(1)} %broadcast_multiply_fusion.2, f32[512]{0:T(512)S(1)} %copy-done.4, ...), kind=kLoop, calls=%fused_computation.8 | loop fusion | flops 22057984 | bytes 16826368 | tf_op jit(solution)/shard_map/reduce_sum | solution.py:81
  169.4 1.4 fusion.14
  170.8 109.2 %all-reduce.4 = (f32[10,512]{1,0:T(8,128)}, f32[2,512]{1,0:T(2,128)}) all-reduce(f32[10,512]{1,0:T(8,128)S(1)} %fusion.14, f32[2,512]{1,0:T(2,128)S(1)} %pad_maximum_fusion.8), channel_id=1, replica_groups=mesh['dx'=16,'dy'=32] {'dx','dy'}, use_global_device_ids=true, to_apply=%region_6.7 | all-reduce | flops 6144 | bytes 49152 | tf_op jit(solution)/shard_map/psum | solution.py:115
  279.9 352.6 %all-reduce.7.cloned.1.call-done = f32[1536,512]{1,0:T(8,128)} async-done(((f32[1536,512]{1,0:T(8,128)}), f32[1536,512]{1,0:T(8,128)}) %all-reduce.7.cloned.1.call-update) | async-done | bytes 3145744 | tf_op jit(solution)/shard_map/psum | solution.py:115
  632.5 1.5 constant_dynamic-slice_fusion
  (55 shorter events, 0.5 us)
Async XLA Ops:
  7.2 121.1 %copy-start = (bf16[1536,512]{1,0:T(8,128)(2,1)S(1)}, bf16[1536,512]{1,0:T(8,128)(2,1)}, u32[]{:S(2)}) copy-start(bf16[1536,512]{1,0:T(8,128)(2,1)} %param.13) | copy-start | bytes 4718596
  7.2 31.9 %copy-start.3 = (bf16[1,8,2570]{2,1,0:T(8,128)(2,1)S(1)}, bf16[1,8,2570]{2,1,0:T(8,128)(2,1)}, u32[]{:S(2)}) copy-start(bf16[1,8,2570]{2,1,0:T(8,128)(2,1)} %param.7) | copy-start | bytes 123364
  7.2 625.3 %all-reduce.7.cloned.1.call-start = ((), (), s32[]{:S(2)}) async-start(), calls=%async_computation | async-start | bytes 6291456 | tf_op jit(solution)/shard_map/psum | solution.py:115
  7.2 32.2 %collective-permute-start.1 = (bf16[1,8,2570]{2,1,0:T(8,128)(2,1)}, bf16[1,8,2570]{2,1,0:T(8,128)(2,1)S(1)}, u32[]{:S(2)}, u32[]{:S(2)}) collective-permute-start(bf16[1,8,2570]{2,1,0:T(8,128)(2,1)} %param.7), channel_id=1, source_target_pairs={{0,480},{32,0},{64,32},{96,64},{128,96},{160,128},{192,160},{224,1... | collective-permute-start | bytes 123368 | tf_op jit(solution)/shard_map/ppermute | solution.py:22
  17.8 24.2 %collective-permute-start = (bf16[1,8,2570]{2,1,0:T(8,128)(2,1)}, bf16[1,8,2570]{2,1,0:T(8,128)(2,1)S(1)}, u32[]{:S(2)}, u32[]{:S(2)}) collective-permute-start(bf16[1,8,2570]{2,1,0:T(8,128)(2,1)} %param.7), channel_id=1, source_target_pairs={{0,32},{32,64},{64,96},{96,128},{128,160},{160,192},{192,224},{224... | collective-permute-start | bytes 123368 | tf_op jit(solution)/shard_map/ppermute | solution.py:17
  36.1 69.7 %copy-start.5 = (bf16[10,512]{1,0:T(8,128)(2,1)S(1)}, bf16[10,512]{1,0:T(8,128)(2,1)}, u32[]{:S(2)}) copy-start(bf16[10,512]{1,0:T(8,128)(2,1)} %param.10) | copy-start | bytes 30724
  39.4 6.1 collective-permute-start.3
  42.0 6.3 collective-permute-start.2
  45.5 5.9 collective-permute-start.5
  48.3 8.8 %collective-permute-start.4 = (bf16[1,8,2570]{2,1,0:T(8,128)(2,1)S(1)}, bf16[1,8,2570]{2,1,0:T(8,128)(2,1)S(1)}, u32[]{:S(2)}, u32[]{:S(2)}) collective-permute-start(bf16[1,8,2570]{2,1,0:T(8,128)(2,1)S(1)} %collective-permute-done.2), channel_id=1, source_target_pairs={{0,32},{32,64},{64,96},{96,128},{128,160},{160,192},{192,224},{224... | collective-permute-start | bytes 123368 | tf_op jit(solution)/shard_map/ppermute | solution.py:17
  51.4 7.7 %collective-permute-start.7 = (bf16[1,8,2570]{2,1,0:T(8,128)(2,1)S(1)}, bf16[1,8,2570]{2,1,0:T(8,128)(2,1)S(1)}, u32[]{:S(2)}, u32[]{:S(2)}) collective-permute-start(bf16[1,8,2570]{2,1,0:T(8,128)(2,1)S(1)} %collective-permute-done.5), channel_id=1, source_target_pairs={{0,480},{32,0},{64,32},{96,64},{128,96},{160,128},{192,160},{224,1... | collective-permute-start | bytes 123368 | tf_op jit(solution)/shard_map/ppermute | solution.py:22
  57.1 9.2 %collective-permute-start.6 = (bf16[1,8,2570]{2,1,0:T(8,128)(2,1)S(1)}, bf16[1,8,2570]{2,1,0:T(8,128)(2,1)S(1)}, u32[]{:S(2)}, u32[]{:S(2)}) collective-permute-start(bf16[1,8,2570]{2,1,0:T(8,128)(2,1)S(1)} %collective-permute-done.4), channel_id=1, source_target_pairs={{0,32},{32,64},{64,96},{96,128},{128,160},{160,192},{192,224},{224... | collective-permute-start | bytes 123368 | tf_op jit(solution)/shard_map/ppermute | solution.py:17
  59.1 9.2 %collective-permute-start.9 = (bf16[1,8,2570]{2,1,0:T(8,128)(2,1)S(1)}, bf16[1,8,2570]{2,1,0:T(8,128)(2,1)S(1)}, u32[]{:S(2)}, u32[]{:S(2)}) collective-permute-start(bf16[1,8,2570]{2,1,0:T(8,128)(2,1)S(1)} %collective-permute-done.7), channel_id=1, source_target_pairs={{0,480},{32,0},{64,32},{96,64},{128,96},{160,128},{192,160},{224,1... | collective-permute-start | bytes 123368 | tf_op jit(solution)/shard_map/ppermute | solution.py:22
  66.4 9.7 %collective-permute-start.8 = (bf16[1,8,2570]{2,1,0:T(8,128)(2,1)S(1)}, bf16[1,8,2570]{2,1,0:T(8,128)(2,1)S(1)}, u32[]{:S(2)}, u32[]{:S(2)}) collective-permute-start(bf16[1,8,2570]{2,1,0:T(8,128)(2,1)S(1)} %collective-permute-done.6), channel_id=1, source_target_pairs={{0,32},{32,64},{64,96},{96,128},{128,160},{160,192},{192,224},{224... | collective-permute-start | bytes 123368 | tf_op jit(solution)/shard_map/ppermute | solution.py:17
  68.4 9.6 %collective-permute-start.11 = (bf16[1,8,2570]{2,1,0:T(8,128)(2,1)S(1)}, bf16[1,8,2570]{2,1,0:T(8,128)(2,1)S(1)}, u32[]{:S(2)}, u32[]{:S(2)}) collective-permute-start(bf16[1,8,2570]{2,1,0:T(8,128)(2,1)S(1)} %collective-permute-done.9), channel_id=1, source_target_pairs={{0,480},{32,0},{64,32},{96,64},{128,96},{160,128},{192,160},{224,1... | collective-permute-start | bytes 123368 | tf_op jit(solution)/shard_map/ppermute | solution.py:22
  76.0 9.2 %collective-permute-start.10 = (bf16[1,8,2570]{2,1,0:T(8,128)(2,1)S(1)}, bf16[1,8,2570]{2,1,0:T(8,128)(2,1)S(1)}, u32[]{:S(2)}, u32[]{:S(2)}) collective-permute-start(bf16[1,8,2570]{2,1,0:T(8,128)(2,1)S(1)} %collective-permute-done.8), channel_id=1, source_target_pairs={{0,32},{32,64},{64,96},{96,128},{128,160},{160,192},{192,224},{224... | collective-permute-start | bytes 123368 | tf_op jit(solution)/shard_map/ppermute | solution.py:17
  78.0 18.4 %collective-permute-start.13 = (bf16[1,8,2570]{2,1,0:T(8,128)(2,1)S(1)}, bf16[1,8,2570]{2,1,0:T(8,128)(2,1)S(1)}, u32[]{:S(2)}, u32[]{:S(2)}) collective-permute-start(bf16[1,8,2570]{2,1,0:T(8,128)(2,1)S(1)} %collective-permute-done.11), channel_id=1, source_target_pairs={{0,480},{32,0},{64,32},{96,64},{128,96},{160,128},{192,160},{224,1... | collective-permute-start | bytes 123368 | tf_op jit(solution)/shard_map/ppermute | solution.py:22
  85.3 9.2 %collective-permute-start.12 = (bf16[1,8,2570]{2,1,0:T(8,128)(2,1)S(1)}, bf16[1,8,2570]{2,1,0:T(8,128)(2,1)S(1)}, u32[]{:S(2)}, u32[]{:S(2)}) collective-permute-start(bf16[1,8,2570]{2,1,0:T(8,128)(2,1)S(1)} %collective-permute-done.10), channel_id=1, source_target_pairs={{0,32},{32,64},{64,96},{96,128},{128,160},{160,192},{192,224},{224... | collective-permute-start | bytes 123368 | tf_op jit(solution)/shard_map/ppermute | solution.py:17
  94.5 9.2 %collective-permute-start.14 = (bf16[1,8,2570]{2,1,0:T(8,128)(2,1)S(1)}, bf16[1,8,2570]{2,1,0:T(8,128)(2,1)S(1)}, u32[]{:S(2)}, u32[]{:S(2)}) collective-permute-start(bf16[1,8,2570]{2,1,0:T(8,128)(2,1)S(1)} %collective-permute-done.12), channel_id=1, source_target_pairs={{0,32},{32,64},{64,96},{96,128},{128,160},{160,192},{192,224},{224... | collective-permute-start | bytes 123368 | tf_op jit(solution)/shard_map/ppermute | solution.py:17
  105.9 2.8 copy-start.4
  105.9 2.8 copy-start.6
  106.6 2.0 copy-start.1
  128.3 5.7 copy-start.2
  133.1 1.0 copy-start.7
  155.9 13.5 %slice-start = ((s8[4259840]{0:T(1024)(128)(4,1)}), s8[65536]{0:T(1024)(128)(4,1)S(1)}, s32[]{:S(2)}) async-start(s8[4259840]{0:T(1024)(128)(4,1)} %bitcast.79), calls=%async_computation.1 | async-start | bytes 131072
  162.0 7.4 %slice-start.1 = ((s8[4259840]{0:T(1024)(128)(4,1)}), s8[4194304]{0:T(1024)(128)(4,1)S(1)}, s32[]{:S(2)}) async-start(s8[4259840]{0:T(1024)(128)(4,1)} %bitcast.79), calls=%async_computation.2 | async-start | bytes 8388608
Sparse Core Ops, SparseCore 0:
  144.6 487.8 all-reduce.6
